TPU v7x, 32 devices: a whole 2x2x4 slice. The times are simulated.
32 devices in a mesh: seq: 8 (over z, y), chan: 4 (over x, core).
Axes of the slice: x: 2, y: 2, z: 4, core: 2. Of those that a mesh axis runs over, the one named last changes fastest.
Arguments:
- query_proj: bfloat16 [1024, 4096], P('seq', 'chan'), may hold values from -6 to 6
- key_proj: bfloat16 [1024, 4096], P('seq', 'chan'), may hold values from -6 to 6
- value_proj: bfloat16 [1024, 4096], P('seq', 'chan'), may hold values from -6 to 6
- short_taps: float32 [3, 3, 4096], P(None, None, 'chan'), may hold values from -2.5 to 2.5
- skip_gain: float32 [4096], P('chan'), may hold values from 0.5 to 1.5
- long_filter: float32 [4096, 1024], P(('chan', 'seq')), may hold values from -1024 to 1024
- out_grad: bfloat16 [1024, 4096], P('seq', 'chan'), may hold values from -6 to 6
Outputs:
- mixed_out: bfloat16 [1024, 4096], P('seq', 'chan')
- query_grad: bfloat16 [1024, 4096], P('seq', 'chan')
- key_grad: bfloat16 [1024, 4096], P('seq', 'chan')
- value_grad: bfloat16 [1024, 4096], P('seq', 'chan')
- filter_grad: float32 [4096, 1024], P(('chan', 'seq'))
All inputs are finite; a program needn't handle non-finite values.
Results may differ from a plain program's by a relative error of at most 0.0075.
Values may be sent and summed in bfloat16 or wider, within the bound.
A program may use at most 64 MiB of HBM per device.

v0:
```python
import functools
import math

import jax
import jax.numpy as jnp
import ml_dtypes
import numpy as np
from jax import lax
from jax.experimental import pallas as pl
from jax.experimental.pallas import tpu as pltpu
from jax.sharding import PartitionSpec as P

F32 = jnp.float32
BF16 = jnp.bfloat16
BLOCK = 128


def transform_tables(length):
    odd = 2 * np.arange(length, dtype=np.int64) + 1
    counts = odd[:, None] * np.arange(length, dtype=np.int64)[None, :] % (4 * length)
    angles = counts * (math.pi / (2 * length))
    forward = np.concatenate([np.cos(angles), np.sin(angles)], 0)
    forward = forward.astype(ml_dtypes.bfloat16)
    return forward, np.ascontiguousarray(forward.T)


def dense_kernel(
    n_seq,
    n_chan,
    query_ref,
    key_ref,
    value_ref,
    taps_ref,
    skip_ref,
    filter_ref,
    cotangent_ref,
    forward_hbm,
    inverse_hbm,
    mixed_ref,
    query_grad_ref,
    key_grad_ref,
    value_grad_ref,
    filter_grad_ref,
    forward,
    inverse,
    extended,
    shorted,
    gated,
    halo_out,
    halo_in,
    block_out,
    block_in,
    result_out,
    result_in,
    filter_out,
    filter_in,
    skip_in,
    terms_out,
    terms_in,
    spectra,
    products,
    even_part,
    odd_part,
    lag_spectra,
    halo_sent,
    halo_got,
    block_sent,
    block_got,
    result_sent,
    result_got,
    single_sent,
    single_got,
    table_got,
):
    rows = query_ref.shape[0]
    length = filter_ref.shape[1]
    chunk = 2 * rows
    chunks = length // chunk
    me = lax.axis_index("seq")
    chan = lax.axis_index("chan")
    is_owner = chan % 2 == 0
    not_owner = chan % 2 == 1
    owner_chan = jnp.where(is_owner, chan, n_chan - 1 - chan)
    other_chan = n_chan - 1 - owner_chan
    side = chan % 2
    mirrored_seq = n_seq - 1 - me

    def device(seq, chan_index):
        return {"seq": seq, "chan": chan_index}

    def remote(source, target, sent, got, where):
        return pltpu.make_async_remote_copy(
            src_ref=source,
            dst_ref=target,
            send_sem=sent,
            recv_sem=got,
            device_id=where,
            device_id_type=pl.DeviceIdType.MESH,
        )

    def await_on(buffer, semaphore):
        pltpu.make_async_copy(buffer, buffer, semaphore).wait()

    def lanes_of(block):
        return pl.ds(pl.multiple_of(block * BLOCK, BLOCK), BLOCK)

    forward_copy = pltpu.make_async_copy(forward_hbm, forward, table_got.at[0])
    inverse_copy = pltpu.make_async_copy(inverse_hbm, inverse, table_got.at[1])

    barrier = pltpu.get_barrier_semaphore()

    def greet(index, carry):
        seq = index % n_seq
        target = jnp.where(index < n_seq, owner_chan, other_chan)

        @pl.when(jnp.logical_or(seq != me, target != chan))
        def _():
            pl.semaphore_signal(
                barrier,
                inc=1,
                device_id=device(seq, target),
                device_id_type=pl.DeviceIdType.MESH,
            )

        return carry

    lax.fori_loop(0, 2 * n_seq, greet, 0)

    @pl.when(is_owner)
    def _():
        forward_copy.start()
        inverse_copy.start()

    sources = (query_ref, key_ref, value_ref)
    for p in range(3):
        extended[p, 8 : rows + 8, :] = sources[p][...].astype(F32)
    extended[3, 8 : rows + 8, :] = cotangent_ref[...].astype(F32)
    halo_out[0] = jnp.concatenate([extended[p, rows + 6 : rows + 8, :] for p in range(4)], 0)
    halo_out[1] = jnp.concatenate([extended[p, 8:10, :] for p in range(4)], 0)

    pl.semaphore_wait(barrier, 2 * n_seq - 1)

    to_next = remote(
        halo_out.at[0],
        halo_in.at[0],
        halo_sent.at[0],
        halo_got.at[0],
        device(jnp.minimum(me + 1, n_seq - 1), chan),
    )
    to_previous = remote(
        halo_out.at[1],
        halo_in.at[1],
        halo_sent.at[1],
        halo_got.at[1],
        device(jnp.maximum(me - 1, 0), chan),
    )

    @pl.when(me < n_seq - 1)
    def _():
        to_next.start()

    @pl.when(me > 0)
    def _():
        to_previous.start()

    @pl.when(not_owner)
    def _():
        filter_out[...] = filter_ref[...].astype(BF16)

    @pl.when(me > 0)
    def _():
        await_on(halo_in.at[0], halo_got.at[0])

    @pl.when(me == 0)
    def _():
        halo_in[0] = jnp.zeros(halo_in.shape[1:], F32)

    @pl.when(me < n_seq - 1)
    def _():
        await_on(halo_in.at[1], halo_got.at[1])

    @pl.when(me == n_seq - 1)
    def _():
        halo_in[1] = jnp.zeros(halo_in.shape[1:], F32)

    for p in range(4):
        extended[p, 6:8, :] = halo_in[0, 2 * p : 2 * p + 2, :]
        extended[p, rows + 8 : rows + 16, :] = jnp.concatenate(
            [halo_in[1, 2 * p : 2 * p + 2, :], jnp.zeros((6, halo_in.shape[2]), F32)], 0
        )

    def owner_of(block):
        return jnp.where(is_owner, block, n_seq - 1 - block)

    def send_block(step, carry):
        block = (me + n_seq // 2 + step) % n_seq
        lanes = lanes_of(block)
        for p in range(3):
            total = taps_ref[p, 0:1, lanes] * extended[p, 8 : rows + 16, lanes]
            total += taps_ref[p, 1:2, lanes] * extended[p, 7 : rows + 15, lanes]
            total += taps_ref[p, 2:3, lanes] * extended[p, 6 : rows + 14, lanes]
            shorted[p, :, lanes] = total.astype(BF16).astype(F32)
        product = shorted[1, 0:rows, lanes] * shorted[2, 0:rows, lanes]
        block_out[block, 0:rows, :] = product.astype(BF16)
        gate = extended[3, 8 : rows + 8, lanes] * shorted[0, 0:rows, lanes]
        block_out[block, rows : 2 * rows, :] = gate.astype(BF16)
        target = owner_of(block)
        here = jnp.logical_and(is_owner, block == me)

        @pl.when(here)
        def _():
            pltpu.make_async_copy(
                block_out.at[block], block_in.at[0, me], block_got.at[0, me]
            ).start()

        @pl.when(jnp.logical_not(here))
        def _():
            remote(
                block_out.at[block],
                block_in.at[side, me],
                block_sent.at[block],
                block_got.at[side, me],
                device(target, owner_chan),
            ).start()

        return carry

    lax.fori_loop(0, n_seq, send_block, 0)

    filter_copy = remote(
        filter_out,
        filter_in,
        single_sent.at[0],
        single_got.at[0],
        device(mirrored_seq, owner_chan),
    )
    skip_copy = remote(
        skip_ref, skip_in, single_sent.at[1], single_got.at[1], device(mirrored_seq, owner_chan)
    )
    terms_copy = remote(
        terms_out, terms_in, single_sent.at[2], single_got.at[2], device(mirrored_seq, other_chan)
    )

    @pl.when(not_owner)
    def _():
        skip_copy.start()
        filter_copy.start()

    def columns_of(seq):
        return jnp.concatenate(
            [
                block_in[0, seq, 0:rows, :],
                block_in[1, seq, 0:rows, :],
                block_in[0, seq, rows : 2 * rows, :],
                block_in[1, seq, rows : 2 * rows, :],
            ],
            1,
        )

    wide = 2 * BLOCK

    @pl.when(is_owner)
    def _():
        forward_copy.wait()
        for step in range(chunks):
            piece = (me // 2 + step) % chunks
            for half in range(2):
                for from_side in range(2):
                    seq = 2 * piece + half
                    await_on(block_in.at[from_side, seq], block_got.at[from_side, seq])
            columns = jnp.concatenate([columns_of(2 * piece), columns_of(2 * piece + 1)], 0)
            lags = pl.ds(pl.multiple_of(piece * chunk, chunk), chunk)

            def transform(index, carry):
                at = pl.ds(pl.multiple_of(index * chunk, chunk), chunk)
                term = jnp.dot(forward[at, lags], columns, preferred_element_type=F32)
                if step == 0:
                    spectra[at, :] = term
                else:
                    spectra[at, :] += term
                return carry

            lax.fori_loop(0, 2 * chunks, transform, 0)

        down = lax.broadcasted_iota(jnp.int32, (BLOCK, BLOCK), 0)
        across = lax.broadcasted_iota(jnp.int32, (BLOCK, BLOCK), 1)
        flip = jnp.where(down + across == BLOCK - 1, 1.0, 0.0).astype(BF16)

        def flipped(values):
            return jnp.dot(flip, values, preferred_element_type=F32)

        def halves(index):
            start = pl.multiple_of(index * chunk, chunk)
            return pl.ds(start, chunk), pl.ds(length + start, chunk)

        def lag_products(index, carry):
            first, second = halves(index)
            input_cos, input_sin = spectra[first, 0:wide], spectra[second, 0:wide]
            grad_cos, grad_sin = spectra[first, wide:], spectra[second, wide:]
            real = input_cos * grad_cos + input_sin * grad_sin
            imag = input_sin * grad_cos - input_cos * grad_sin
            lag_spectra[:, first] = real.T.astype(BF16)
            lag_spectra[:, second] = imag.T.astype(BF16)
            return carry

        lax.fori_loop(0, chunks, lag_products, 0)
        scale = 1.0 / (length * math.sqrt(length))

        def filter_terms(index, carry):
            lags = pl.ds(pl.multiple_of(index * chunk, chunk), chunk)
            cosine = jnp.dot(
                lag_spectra[:, 0:length], forward[0:length, lags], preferred_element_type=F32
            )
            sine = jnp.dot(
                lag_spectra[:, length:], forward[length:, lags], preferred_element_type=F32
            )
            ahead = cosine - sine
            behind = (cosine + sine).astype(BF16)
            terms_out[:, lags] = ((ahead[BLOCK:] + flipped(behind[:BLOCK])) * scale).astype(BF16)
            filter_grad_ref[:, lags] = (ahead[:BLOCK] + flipped(behind[BLOCK:])) * scale
            return carry

        lax.fori_loop(0, chunks, filter_terms, 0)
        terms_copy.start()

        await_on(filter_in, single_got.at[0])
        own = filter_ref[...]
        other = filter_in[...]
        own_flipped = flipped(own.astype(BF16))
        other_flipped = flipped(other)
        other = other.astype(F32)
        even_part[0:BLOCK, :] = (own + other_flipped).astype(BF16)
        even_part[BLOCK:, :] = (other + own_flipped).astype(BF16)
        odd_part[0:BLOCK, :] = (own - other_flipped).astype(BF16)
        odd_part[BLOCK:, :] = (other - own_flipped).astype(BF16)

        def spectral_products(index, carry):
            first, second = halves(index)
            contracted = (((1,), (1,)), ((), ()))
            kernel_cos = lax.dot_general(
                forward[first, :], even_part[...], contracted, preferred_element_type=F32
            )
            kernel_sin = lax.dot_general(
                forward[second, :], odd_part[...], contracted, preferred_element_type=F32
            )
            input_cos, input_sin = spectra[first, 0:wide], spectra[second, 0:wide]
            grad_cos, grad_sin = spectra[first, wide:], spectra[second, wide:]
            mix_cos = kernel_cos * input_cos - kernel_sin * input_sin
            mix_sin = kernel_cos * input_sin + kernel_sin * input_cos
            back_cos = kernel_cos * grad_cos + kernel_sin * grad_sin
            back_sin = kernel_cos * grad_sin - kernel_sin * grad_cos
            products[first, 0:wide] = mix_cos.astype(BF16)
            products[second, 0:wide] = mix_sin.astype(BF16)
            products[first, wide:] = back_cos.astype(BF16)
            products[second, wide:] = back_sin.astype(BF16)
            return carry

        lax.fori_loop(0, chunks, spectral_products, 0)
        await_on(skip_in, single_got.at[1])
        gains = [skip_ref[pl.ds(me, 1), :], skip_in[pl.ds(mirrored_seq, 1), :]]
        gains = jnp.concatenate(gains + gains, 1)
        inverse_copy.wait()

        def results(index, carry):
            at = pl.ds(pl.multiple_of(index * chunk, chunk), chunk)
            sums = jnp.dot(inverse[at, :], products[...], preferred_element_type=F32) * scale
            for half in range(2):
                seq = 2 * index + half
                here = sums[half * rows : (half + 1) * rows]
                here = here + gains * columns_of(seq).astype(F32)
                before = (seq + n_seq - 1) % n_seq
                kept = jnp.where(seq > 0, 1.0, 0.0)
                for to_side in range(2):
                    mix = here[:, to_side * BLOCK : (to_side + 1) * BLOCK]
                    back = here[:, wide + to_side * BLOCK : wide + (to_side + 1) * BLOCK]
                    result_out[to_side, seq, 0:rows, :] = mix.astype(BF16)
                    result_out[to_side, seq, rows : 2 * rows, :] = back.astype(BF16)
                    edge = jnp.concatenate([mix[0:2], back[0:2], jnp.zeros((12, BLOCK), F32)], 0)
                    result_out[to_side, before, 2 * rows :, :] = (edge * kept).astype(BF16)
            return carry

        lax.fori_loop(0, chunks, results, 0)

        def send_result(step, carry):
            seq = (me + n_seq // 2 + step) % n_seq

            remote(
                result_out.at[1, seq],
                result_in.at[mirrored_seq],
                result_sent.at[1, seq],
                result_got.at[mirrored_seq],
                device(seq, other_chan),
            ).start()

            @pl.when(seq == me)
            def _():
                pltpu.make_async_copy(
                    result_out.at[0, me], result_in.at[me], result_got.at[me]
                ).start()

            @pl.when(seq != me)
            def _():
                remote(
                    result_out.at[0, seq],
                    result_in.at[me],
                    result_sent.at[0, seq],
                    result_got.at[me],
                    device(seq, owner_chan),
                ).start()

            return carry

        lax.fori_loop(0, n_seq, send_result, 0)

    def finish_block(step, carry):
        source = (me + n_seq // 2 + n_seq - step) % n_seq
        block = owner_of(source)
        lanes = lanes_of(block)
        await_on(result_in.at[block], result_got.at[block])
        edge = result_in[block, 2 * rows :, :].astype(F32)
        mix = result_in[block, 0:rows, :].astype(F32)
        back = result_in[block, rows : 2 * rows, :].astype(F32)
        spare = jnp.zeros((6, BLOCK), F32)
        mixed_ref[:, lanes] = (shorted[0, 0:rows, lanes] * mix).astype(BF16)
        mix = jnp.concatenate([mix, edge[0:2], spare], 0)
        back = jnp.concatenate([back, edge[2:4], spare], 0)
        gated[0] = extended[3, 8 : rows + 16, lanes] * mix
        gated[1] = back * shorted[2, :, lanes]
        gated[2] = back * shorted[1, :, lanes]
        for p, target in enumerate((query_grad_ref, key_grad_ref, value_grad_ref)):
            total = taps_ref[p, 0:1, lanes] * gated[p, 0:rows, :]
            total += taps_ref[p, 1:2, lanes] * gated[p, 1 : rows + 1, :]
            total += taps_ref[p, 2:3, lanes] * gated[p, 2 : rows + 2, :]
            target[:, lanes] = total.astype(BF16)
        return carry

    lax.fori_loop(0, n_seq, finish_block, 0)

    @pl.when(not_owner)
    def _():
        await_on(terms_in, single_got.at[2])
        filter_grad_ref[...] = terms_in[...].astype(F32)
        filter_copy.wait_send()
        skip_copy.wait_send()

    @pl.when(me < n_seq - 1)
    def _():
        to_next.wait_send()

    @pl.when(me > 0)
    def _():
        to_previous.wait_send()

    def drain_block(block, carry):
        @pl.when(jnp.logical_or(not_owner, block != me))
        def _():
            await_on(block_out.at[block], block_sent.at[block])

        return carry

    lax.fori_loop(0, n_seq, drain_block, 0)

    @pl.when(is_owner)
    def _():
        terms_copy.wait_send()

        def drain_result(seq, carry):
            await_on(result_out.at[1, seq], result_sent.at[1, seq])

            @pl.when(seq != me)
            def _():
                await_on(result_out.at[0, seq], result_sent.at[0, seq])

            return carry

        lax.fori_loop(0, n_seq, drain_result, 0)


def dense_device(
    n_seq, n_chan, tables, query, key, value, short_taps, skip_gain, long_filter, cotangent
):
    rows, width = query.shape
    channels, length = long_filter.shape
    whole = pl.BlockSpec(memory_space=pltpu.VMEM)
    apart = pl.BlockSpec(memory_space=pl.ANY)
    sequence_like = jax.ShapeDtypeStruct((rows, width), BF16)
    wide = 2 * channels
    semaphores = pltpu.SemaphoreType.DMA
    return pl.pallas_call(
        functools.partial(dense_kernel, n_seq, n_chan),
        out_shape=(sequence_like,) * 4 + (jax.ShapeDtypeStruct((channels, length), F32),),
        in_specs=[whole] * 7 + [apart] * 2,
        out_specs=(whole,) * 5,
        scratch_shapes=[
            pltpu.VMEM((2 * length, length), BF16),
            pltpu.VMEM((length, 2 * length), BF16),
            pltpu.VMEM((4, rows + 16, width), F32),
            pltpu.VMEM((3, rows + 8, width), F32),
            pltpu.VMEM((3, rows + 8, channels), F32),
            pltpu.VMEM((2, 8, width), F32),
            pltpu.VMEM((2, 8, width), F32),
            pltpu.VMEM((n_seq, 2 * rows, channels), BF16),
            pltpu.VMEM((2, n_seq, 2 * rows, channels), BF16),
            pltpu.VMEM((2, n_seq, 2 * rows + 16, channels), BF16),
            pltpu.VMEM((n_seq, 2 * rows + 16, channels), BF16),
            pltpu.VMEM((channels, length), BF16),
            pltpu.VMEM((channels, length), BF16),
            pltpu.VMEM((n_seq, channels), F32),
            pltpu.VMEM((channels, length), BF16),
            pltpu.VMEM((channels, length), BF16),
            pltpu.VMEM((2 * length, 2 * wide), F32),
            pltpu.VMEM((2 * length, 2 * wide), BF16),
            pltpu.VMEM((wide, length), BF16),
            pltpu.VMEM((wide, length), BF16),
            pltpu.VMEM((wide, 2 * length), BF16),
            semaphores((2,)),
            semaphores((2,)),
            semaphores((n_seq,)),
            semaphores((2, n_seq)),
            semaphores((2, n_seq)),
            semaphores((n_seq,)),
            semaphores((3,)),
            semaphores((3,)),
            semaphores((2,)),
        ],
        compiler_params=pltpu.CompilerParams(
            collective_id=0, has_side_effects=True, vmem_limit_bytes=56 * 1024 * 1024
        ),
    )(
        query,
        key,
        value,
        short_taps,
        skip_gain.reshape(n_seq, channels),
        long_filter,
        cotangent,
        *[jnp.asarray(table) for table in tables],
    )


exact_mode = lax.Precision.HIGHEST


def from_partner(array, axis, stride):
    return lax.ppermute(array, axis, [(i, i ^ 1 << stride) for i in range(lax.axis_size(axis))])


def passed_along(array, axis, by):
    length = lax.axis_size(axis)
    pairs = [(i, i + by) for i in range(length) if 0 <= i + by < length]
    return lax.ppermute(array, axis, pairs)


def divisor_pair(total_size):
    first_side = 1
    for candidate in range(1, math.isqrt(total_size) + 1):
        if total_size % candidate == 0:
            first_side = candidate
    return (first_side, total_size // first_side)


def angle_table(height, across, period):
    counts = (
        jnp.arange(height, dtype=jnp.int32)[:, None]
        * jnp.arange(across, dtype=jnp.int32)[None, :]
        % period
    )
    angles = counts.astype(jnp.float32) * (2.0 * math.pi / period)
    return (jnp.cos(angles), jnp.sin(angles))


def make_tables(total_size):
    first_side, second_side = divisor_pair(total_size)
    return (
        angle_table(first_side, first_side, first_side),
        angle_table(first_side, second_side, total_size),
        angle_table(second_side, second_side, second_side),
        first_side,
        second_side,
    )


def right_product(values, matrix):
    return jnp.einsum("ckm,ml->ckl", values, matrix, precision=exact_mode)


def left_product(matrix, values):
    return jnp.einsum("kn,cnm->ckm", matrix, values, precision=exact_mode)


def spectrum_of(signal, tables):
    (
        (cos_first, sin_first),
        (cosine_rotation, sin_twist),
        (cos_second, sin_second),
        first_side,
        second_side,
    ) = tables
    shaped = signal.reshape(signal.shape[0], first_side, second_side)
    section_real = left_product(cos_first, shaped)
    section_imag = -left_product(sin_first, shaped)
    twist_real = section_real * cosine_rotation + section_imag * sin_twist
    twist_imag = section_imag * cosine_rotation - section_real * sin_twist
    return (
        right_product(twist_real, cos_second) + right_product(twist_imag, sin_second),
        right_product(twist_imag, cos_second) - right_product(twist_real, sin_second),
    )


def signal_of(spectrum, tables):
    (
        (cos_first, sin_first),
        (cosine_rotation, sin_twist),
        (cos_second, sin_second),
        first_side,
        second_side,
    ) = tables
    spec_real, spec_imag = spectrum
    section_real = right_product(spec_real, cos_second) - right_product(spec_imag, sin_second)
    section_imag = right_product(spec_imag, cos_second) + right_product(spec_real, sin_second)
    twist_real = section_real * cosine_rotation - section_imag * sin_twist
    twist_imag = section_imag * cosine_rotation + section_real * sin_twist
    result = left_product(cos_first, twist_real) - left_product(sin_first, twist_imag)
    return result.reshape(result.shape[0], -1) / (first_side * second_side)


def times_spec(former, latter):
    return (
        former[0] * latter[0] - former[1] * latter[1],
        former[0] * latter[1] + former[1] * latter[0],
    )


def conj_times(former, latter):
    return (
        former[0] * latter[0] + former[1] * latter[1],
        former[0] * latter[1] - former[1] * latter[0],
    )


def mirror_rows(block_rows):
    mirrored = block_rows
    for bit_index in range((lax.axis_size("seq") * lax.axis_size("chan")).bit_length() - 1):
        mirrored = from_partner(mirrored, ("seq", "chan"), bit_index)
    return mirrored[::-1]


def per_device(query_proj, key_proj, value_proj, short_taps, skip_gain, long_filter, out_grad):
    positions = query_proj.shape[0]
    channels, length = long_filter.shape
    doubled = 2 * length
    factor_root = 1.0 / math.sqrt(length)
    tables = make_tables(doubled)
    own_skip = lax.dynamic_slice_in_dim(skip_gain, lax.axis_index("seq") * channels, channels)[
        :, None
    ]
    stacked = jnp.stack([query_proj, key_proj, value_proj])
    previous = passed_along(stacked[:, positions - 2 :], "seq", 1)
    extended = jnp.concatenate([previous, stacked], 1).astype(jnp.float32)
    tap_rows = short_taps[:, :, None, :]
    shorted = (
        tap_rows[:, 0] * extended[:, 2 : positions + 2]
        + tap_rows[:, 1] * extended[:, 1 : positions + 1]
        + tap_rows[:, 2] * extended[:, 0:positions]
    )
    shorted = shorted.astype(jnp.bfloat16)
    query_short, key_short, value_short = (shorted[0], shorted[1], shorted[2])
    key_wide = key_short.astype(jnp.float32)
    value_wide = value_short.astype(jnp.float32)
    product_in = (key_wide * value_wide).astype(jnp.bfloat16)
    kernel_own = long_filter * factor_root
    kernel_mirror = mirror_rows(kernel_own)
    zero_column = jnp.zeros((channels, 1), jnp.float32)
    kernel_full = jnp.concatenate(
        [
            kernel_own[:, :1] + kernel_mirror[:, :1],
            kernel_own[:, 1:],
            zero_column,
            kernel_mirror[:, 1:][:, ::-1],
        ],
        1,
    )
    spectrum_kernel = spectrum_of(kernel_full, tables)
    query_wide = query_short.astype(jnp.float32)
    chan_product = lax.all_to_all(product_in.T, "seq", split_axis=0, concat_axis=1, tiled=True)
    input_wide = chan_product.astype(jnp.float32)
    input_spectrum = spectrum_of(
        jnp.concatenate([input_wide, jnp.zeros_like(input_wide)], 1), tables
    )
    mixed_wide = signal_of(times_spec(spectrum_kernel, input_spectrum), tables)[:, :length]
    chan_mix, input_spectrum = (
        (mixed_wide + own_skip * input_wide).astype(jnp.bfloat16),
        input_spectrum,
    )
    long_mix = lax.all_to_all(chan_mix, "seq", split_axis=1, concat_axis=0, tiled=True).T
    gate_grad = (out_grad.astype(jnp.float32) * query_wide).astype(jnp.bfloat16)
    chan_gate = lax.all_to_all(gate_grad.T, "seq", split_axis=0, concat_axis=1, tiled=True)
    grad_wide = chan_gate.astype(jnp.float32)
    spectrum_grad = spectrum_of(jnp.concatenate([grad_wide, jnp.zeros_like(grad_wide)], 1), tables)
    back_wide = signal_of(conj_times(spectrum_kernel, spectrum_grad), tables)[:, :length]
    lagged = signal_of(conj_times(input_spectrum, spectrum_grad), tables)
    chan_back, lagged = ((back_wide + own_skip * grad_wide).astype(jnp.bfloat16), lagged)
    input_grad = lax.all_to_all(chan_back, "seq", split_axis=1, concat_axis=0, tiled=True).T
    mix_wide = long_mix.astype(jnp.float32)
    mixed_out = (query_wide * mix_wide).astype(jnp.bfloat16)
    reversed_part = jnp.concatenate([lagged[:, :1], lagged[:, length + 1 :][:, ::-1]], 1)
    filter_grad = (lagged[:, :length] + mirror_rows(reversed_part)) * factor_root
    input_back = input_grad.astype(jnp.float32)
    gated = jnp.stack(
        [out_grad.astype(jnp.float32) * mix_wide, input_back * value_wide, input_back * key_wide]
    )
    following = passed_along(gated[:, :2], "seq", -1)
    widened = jnp.concatenate([gated, following], 1)
    tap_grads = (
        tap_rows[:, 0] * widened[:, 0:positions]
        + tap_rows[:, 1] * widened[:, 1 : positions + 1]
        + tap_rows[:, 2] * widened[:, 2 : positions + 2]
    )
    tap_grads = tap_grads.astype(jnp.bfloat16)
    return (mixed_out, tap_grads[0], tap_grads[1], tap_grads[2], filter_grad)


def solution(mesh):
    in_specs = (
        P("seq", "chan"),
        P("seq", "chan"),
        P("seq", "chan"),
        P(None, None, "chan"),
        P("chan"),
        P(("chan", "seq"), None),
        P("seq", "chan"),
    )
    out_specs = (
        P("seq", "chan"),
        P("seq", "chan"),
        P("seq", "chan"),
        P("seq", "chan"),
        P(("chan", "seq"), None),
    )
    n_seq, n_chan = mesh.shape["seq"], mesh.shape["chan"]

    def on_device(query_proj, key_proj, value_proj, short_taps, skip_gain, long_filter, out_grad):
        arguments = (
            query_proj, key_proj, value_proj, short_taps, skip_gain, long_filter, out_grad
        )
        rows, width = query_proj.shape
        channels, length = long_filter.shape
        if (
            rows == channels == BLOCK
            and n_seq % 2 == 0
            and n_chan % 2 == 0
            and length <= 1024
        ):
            tables = transform_tables(length)
            return dense_device(n_seq, n_chan, tables, *arguments)
        return per_device(*arguments)

    return jax.shard_map(
        on_device, mesh=mesh, in_specs=in_specs, out_specs=out_specs, check_vma=False
    )
```

profile of v0, /device:TPU:0, one launch (start us, length us, event | category | flops | bytes accessed | tf_op | source)
XLA Modules:
  0.0 65.6 jit_solution(4207829908816507682)
XLA Ops:
  0.6 56.4 %shard_map.128 = (bf16[128,1024]{1,0:T(8,128)(2,1)}, bf16[128,1024]{1,0:T(8,128)(2,1)}, bf16[128,1024]{1,0:T(8,128)(2,1)}, bf16[128,1024]{1,0:T(8,128)(2,1)}, f32[128,1024]{1,0:T(8,128)}) custom-call(bf16[128,1024]{1,0:T(8,128)(2,1)} %query_ref.1, bf16[128,1024]{1,0:T(8,128)(2,1)} %key_ref.1, bf16[128,1024]{1,0:T(8,128)(2,1)} %value_ref.1, ...), custom_call_target="tpu_custom_call" | custom-call | tf_op jit(solution)/shard_map/pallas_call | solution.py:489
  57.0 1.7 %copy.19 = bf16[128,1024]{1,0:T(8,128)(2,1)} copy(bf16[128,1024]{1,0:T(8,128)(2,1)} %get-tuple-element.10) | data formatting | bytes 524288
  58.7 1.7 %copy.20 = bf16[128,1024]{1,0:T(8,128)(2,1)} copy(bf16[128,1024]{1,0:T(8,128)(2,1)} %get-tuple-element.11) | data formatting | bytes 524288
  60.4 1.7 %copy.21 = bf16[128,1024]{1,0:T(8,128)(2,1)} copy(bf16[128,1024]{1,0:T(8,128)(2,1)} %get-tuple-element.12) | data formatting | bytes 524288
  62.0 1.7 %copy.22 = bf16[128,1024]{1,0:T(8,128)(2,1)} copy(bf16[128,1024]{1,0:T(8,128)(2,1)} %get-tuple-element.13) | data formatting | bytes 524288
  63.7 1.9 %copy.23 = f32[128,1024]{1,0:T(8,128)} copy(f32[128,1024]{1,0:T(8,128)} %get-tuple-element.14) | data formatting | bytes 1048576
where the time goes:
time: 65.9 us; the launch traced here: 65.6 us
  Pallas kernels  56.4 us (86%)
  local copies, waits for them, and re-layouts  8.56 us (13%)
    pallas_call x1, Pallas kernels, dense_device(): pl.pallas_call(functools.partial(dense_kernel, n_seq, n_chan), out_shape=...  56.4 us
    unnamed x5, local copies, waits for them, and re-layouts  8.56 us

commit v1 on v0

--- a/solution.py
+++ b/solution.py
@@ -27,19 +27,23 @@
 def dense_kernel(
     n_seq,
     n_chan,
-    query_ref,
-    key_ref,
-    value_ref,
+    query_hbm,
+    key_hbm,
+    value_hbm,
     taps_ref,
     skip_ref,
-    filter_ref,
-    cotangent_ref,
+    filter_hbm,
+    cotangent_hbm,
     forward_hbm,
     inverse_hbm,
-    mixed_ref,
-    query_grad_ref,
-    key_grad_ref,
-    value_grad_ref,
+    mixed_hbm,
+    query_grad_hbm,
+    key_grad_hbm,
+    value_grad_hbm,
+    filter_grad_hbm,
+    arguments,
+    filter_ref,
+    outputs,
     filter_grad_ref,
     forward,
     inverse,
@@ -62,6 +66,7 @@
     even_part,
     odd_part,
     lag_spectra,
+    kernel_spectra,
     halo_sent,
     halo_got,
     block_sent,
@@ -71,9 +76,11 @@
     single_sent,
     single_got,
     table_got,
+    argument_got,
+    output_sent,
 ):
-    rows = query_ref.shape[0]
-    length = filter_ref.shape[1]
+    rows = query_hbm.shape[0]
+    length = filter_hbm.shape[1]
     chunk = 2 * rows
     chunks = length // chunk
     me = lax.axis_index("seq")
@@ -107,6 +114,15 @@
     forward_copy = pltpu.make_async_copy(forward_hbm, forward, table_got.at[0])
     inverse_copy = pltpu.make_async_copy(inverse_hbm, inverse, table_got.at[1])
 
+    argument_copies = [
+        pltpu.make_async_copy(source, arguments.at[p], argument_got.at[p])
+        for p, source in enumerate((query_hbm, key_hbm, value_hbm, cotangent_hbm))
+    ]
+    filter_load = pltpu.make_async_copy(filter_hbm, filter_ref, argument_got.at[4])
+    for copy in argument_copies:
+        copy.start()
+    filter_load.start()
+
     barrier = pltpu.get_barrier_semaphore()
 
     def greet(index, carry):
@@ -131,10 +147,9 @@
         forward_copy.start()
         inverse_copy.start()
 
-    sources = (query_ref, key_ref, value_ref)
-    for p in range(3):
-        extended[p, 8 : rows + 8, :] = sources[p][...].astype(F32)
-    extended[3, 8 : rows + 8, :] = cotangent_ref[...].astype(F32)
+    for p in range(4):
+        argument_copies[p].wait()
+        extended[p, 8 : rows + 8, :] = arguments[p].astype(F32)
     halo_out[0] = jnp.concatenate([extended[p, rows + 6 : rows + 8, :] for p in range(4)], 0)
     halo_out[1] = jnp.concatenate([extended[p, 8:10, :] for p in range(4)], 0)
 
@@ -163,9 +178,26 @@
     def _():
         to_previous.start()
 
+    filter_copy = remote(
+        filter_out,
+        filter_in,
+        single_sent.at[0],
+        single_got.at[0],
+        device(mirrored_seq, owner_chan),
+    )
+    skip_copy = remote(
+        skip_ref, skip_in, single_sent.at[1], single_got.at[1], device(mirrored_seq, owner_chan)
+    )
+    terms_copy = remote(
+        terms_out, terms_in, single_sent.at[2], single_got.at[2], device(mirrored_seq, other_chan)
+    )
+
     @pl.when(not_owner)
     def _():
+        skip_copy.start()
+        filter_load.wait()
         filter_out[...] = filter_ref[...].astype(BF16)
+        filter_copy.start()
 
     @pl.when(me > 0)
     def _():
@@ -227,25 +259,6 @@
 
     lax.fori_loop(0, n_seq, send_block, 0)
 
-    filter_copy = remote(
-        filter_out,
-        filter_in,
-        single_sent.at[0],
-        single_got.at[0],
-        device(mirrored_seq, owner_chan),
-    )
-    skip_copy = remote(
-        skip_ref, skip_in, single_sent.at[1], single_got.at[1], device(mirrored_seq, owner_chan)
-    )
-    terms_copy = remote(
-        terms_out, terms_in, single_sent.at[2], single_got.at[2], device(mirrored_seq, other_chan)
-    )
-
-    @pl.when(not_owner)
-    def _():
-        skip_copy.start()
-        filter_copy.start()
-
     def columns_of(seq):
         return jnp.concatenate(
             [
@@ -261,7 +274,44 @@
 
     @pl.when(is_owner)
     def _():
+        scale = 1.0 / (length * math.sqrt(length))
+        down = lax.broadcasted_iota(jnp.int32, (BLOCK, BLOCK), 0)
+        across = lax.broadcasted_iota(jnp.int32, (BLOCK, BLOCK), 1)
+        flip = jnp.where(down + across == BLOCK - 1, 1.0, 0.0).astype(BF16)
+
+        def flipped(values):
+            return jnp.dot(flip, values, preferred_element_type=F32)
+
+        def halves(index):
+            start = pl.multiple_of(index * chunk, chunk)
+            return pl.ds(start, chunk), pl.ds(length + start, chunk)
+
         forward_copy.wait()
+        filter_load.wait()
+        await_on(filter_in, single_got.at[0])
+        own = filter_ref[...]
+        other = filter_in[...]
+        own_flipped = flipped(own.astype(BF16))
+        other_flipped = flipped(other)
+        other = other.astype(F32)
+        even_part[0:BLOCK, :] = (own + other_flipped).astype(BF16)
+        even_part[BLOCK:, :] = (other + own_flipped).astype(BF16)
+        odd_part[0:BLOCK, :] = (own - other_flipped).astype(BF16)
+        odd_part[BLOCK:, :] = (other - own_flipped).astype(BF16)
+
+        def kernel_transform(index, carry):
+            first, second = halves(index)
+            contracted = (((1,), (1,)), ((), ()))
+            kernel_spectra[first, :] = lax.dot_general(
+                forward[first, :], even_part[...], contracted, preferred_element_type=F32
+            )
+            kernel_spectra[second, :] = lax.dot_general(
+                forward[second, :], odd_part[...], contracted, preferred_element_type=F32
+            )
+            return carry
+
+        lax.fori_loop(0, chunks, kernel_transform, 0)
+
         for step in range(chunks):
             piece = (me // 2 + step) % chunks
             for half in range(2):
@@ -282,16 +332,85 @@
 
             lax.fori_loop(0, 2 * chunks, transform, 0)
 
-        down = lax.broadcasted_iota(jnp.int32, (BLOCK, BLOCK), 0)
-        across = lax.broadcasted_iota(jnp.int32, (BLOCK, BLOCK), 1)
-        flip = jnp.where(down + across == BLOCK - 1, 1.0, 0.0).astype(BF16)
-
-        def flipped(values):
-            return jnp.dot(flip, values, preferred_element_type=F32)
-
-        def halves(index):
-            start = pl.multiple_of(index * chunk, chunk)
-            return pl.ds(start, chunk), pl.ds(length + start, chunk)
+        def spectral_products(index, carry):
+            first, second = halves(index)
+            kernel_cos, kernel_sin = kernel_spectra[first, :], kernel_spectra[second, :]
+            input_cos, input_sin = spectra[first, 0:wide], spectra[second, 0:wide]
+            grad_cos, grad_sin = spectra[first, wide:], spectra[second, wide:]
+            mix_cos = kernel_cos * input_cos - kernel_sin * input_sin
+            mix_sin = kernel_cos * input_sin + kernel_sin * input_cos
+            back_cos = kernel_cos * grad_cos + kernel_sin * grad_sin
+            back_sin = kernel_cos * grad_sin - kernel_sin * grad_cos
+            products[first, 0:wide] = mix_cos.astype(BF16)
+            products[second, 0:wide] = mix_sin.astype(BF16)
+            products[first, wide:] = back_cos.astype(BF16)
+            products[second, wide:] = back_sin.astype(BF16)
+            return carry
+
+        lax.fori_loop(0, chunks, spectral_products, 0)
+        await_on(skip_in, single_got.at[1])
+        gains = [skip_ref[pl.ds(me, 1), :], skip_in[pl.ds(mirrored_seq, 1), :]]
+        gains = jnp.concatenate(gains + gains, 1)
+        inverse_copy.wait()
+
+        def send_result(seq):
+            remote(
+                result_out.at[1, seq],
+                result_in.at[mirrored_seq],
+                result_sent.at[1, seq],
+                result_got.at[mirrored_seq],
+                device(seq, other_chan),
+            ).start()
+
+            @pl.when(seq == me)
+            def _():
+                pltpu.make_async_copy(
+                    result_out.at[0, me], result_in.at[me], result_got.at[me]
+                ).start()
+
+            @pl.when(seq != me)
+            def _():
+                remote(
+                    result_out.at[0, seq],
+                    result_in.at[me],
+                    result_sent.at[0, seq],
+                    result_got.at[me],
+                    device(seq, owner_chan),
+                ).start()
+
+        first_piece = (me // 2 + chunks // 2) % chunks
+        for to_side in range(2):
+            result_out[to_side, n_seq - 1, 2 * rows :, :] = jnp.zeros((16, BLOCK), BF16)
+
+        def results(step, carry):
+            index = (first_piece + chunks - step) % chunks
+            at = pl.ds(pl.multiple_of(index * chunk, chunk), chunk)
+            sums = jnp.dot(inverse[at, :], products[...], preferred_element_type=F32) * scale
+            for half in range(2):
+                seq = 2 * index + half
+                here = sums[half * rows : (half + 1) * rows]
+                here = here + gains * columns_of(seq).astype(F32)
+                before = (seq + n_seq - 1) % n_seq
+                for to_side in range(2):
+                    mix = here[:, to_side * BLOCK : (to_side + 1) * BLOCK]
+                    back = here[:, wide + to_side * BLOCK : wide + (to_side + 1) * BLOCK]
+                    result_out[to_side, seq, 0:rows, :] = mix.astype(BF16)
+                    result_out[to_side, seq, rows : 2 * rows, :] = back.astype(BF16)
+                    edge = jnp.concatenate([mix[0:2], back[0:2], jnp.zeros((12, BLOCK), F32)], 0)
+
+                    @pl.when(seq > 0)
+                    def _():
+                        result_out[to_side, before, 2 * rows :, :] = edge.astype(BF16)
+
+            @pl.when(step > 0)
+            def _():
+                send_result(2 * index + 1)
+
+            send_result(2 * index)
+            return carry
+
+        lax.fori_loop(0, chunks, results, 0)
+        send_result(2 * first_piece + 1)
 
         def lag_products(index, carry):
             first, second = halves(index)
@@ -304,8 +423,6 @@
             return carry
 
         lax.fori_loop(0, chunks, lag_products, 0)
-        scale = 1.0 / (length * math.sqrt(length))
-
         def filter_terms(index, carry):
             lags = pl.ds(pl.multiple_of(index * chunk, chunk), chunk)
             cosine = jnp.dot(
@@ -323,97 +440,15 @@
         lax.fori_loop(0, chunks, filter_terms, 0)
         terms_copy.start()
 
-        await_on(filter_in, single_got.at[0])
-        own = filter_ref[...]
-        other = filter_in[...]
-        own_flipped = flipped(own.astype(BF16))
-        other_flipped = flipped(other)
-        other = other.astype(F32)
-        even_part[0:BLOCK, :] = (own + other_flipped).astype(BF16)
-        even_part[BLOCK:, :] = (other + own_flipped).astype(BF16)
-        odd_part[0:BLOCK, :] = (own - other_flipped).astype(BF16)
-        odd_part[BLOCK:, :] = (other - own_flipped).astype(BF16)
-
-        def spectral_products(index, carry):
-            first, second = halves(index)
-            contracted = (((1,), (1,)), ((), ()))
-            kernel_cos = lax.dot_general(
-                forward[first, :], even_part[...], contracted, preferred_element_type=F32
-            )
-            kernel_sin = lax.dot_general(
-                forward[second, :], odd_part[...], contracted, preferred_element_type=F32
-            )
-            input_cos, input_sin = spectra[first, 0:wide], spectra[second, 0:wide]
-            grad_cos, grad_sin = spectra[first, wide:], spectra[second, wide:]
-            mix_cos = kernel_cos * input_cos - kernel_sin * input_sin
-            mix_sin = kernel_cos * input_sin + kernel_sin * input_cos
-            back_cos = kernel_cos * grad_cos + kernel_sin * grad_sin
-            back_sin = kernel_cos * grad_sin - kernel_sin * grad_cos
-            products[first, 0:wide] = mix_cos.astype(BF16)
-            products[second, 0:wide] = mix_sin.astype(BF16)
-            products[first, wide:] = back_cos.astype(BF16)
-            products[second, wide:] = back_sin.astype(BF16)
-            return carry
-
-        lax.fori_loop(0, chunks, spectral_products, 0)
-        await_on(skip_in, single_got.at[1])
-        gains = [skip_ref[pl.ds(me, 1), :], skip_in[pl.ds(mirrored_seq, 1), :]]
-        gains = jnp.concatenate(gains + gains, 1)
-        inverse_copy.wait()
-
-        def results(index, carry):
-            at = pl.ds(pl.multiple_of(index * chunk, chunk), chunk)
-            sums = jnp.dot(inverse[at, :], products[...], preferred_element_type=F32) * scale
-            for half in range(2):
-                seq = 2 * index + half
-                here = sums[half * rows : (half + 1) * rows]
-                here = here + gains * columns_of(seq).astype(F32)
-                before = (seq + n_seq - 1) % n_seq
-                kept = jnp.where(seq > 0, 1.0, 0.0)
-                for to_side in range(2):
-                    mix = here[:, to_side * BLOCK : (to_side + 1) * BLOCK]
-                    back = here[:, wide + to_side * BLOCK : wide + (to_side + 1) * BLOCK]
-                    result_out[to_side, seq, 0:rows, :] = mix.astype(BF16)
-                    result_out[to_side, seq, rows : 2 * rows, :] = back.astype(BF16)
-                    edge = jnp.concatenate([mix[0:2], back[0:2], jnp.zeros((12, BLOCK), F32)], 0)
-                    result_out[to_side, before, 2 * rows :, :] = (edge * kept).astype(BF16)
-            return carry
-
-        lax.fori_loop(0, chunks, results, 0)
-
-        def send_result(step, carry):
-            seq = (me + n_seq // 2 + step) % n_seq
-
-            remote(
-                result_out.at[1, seq],
-                result_in.at[mirrored_seq],
-                result_sent.at[1, seq],
-                result_got.at[mirrored_seq],
-                device(seq, other_chan),
-            ).start()
-
-            @pl.when(seq == me)
-            def _():
-                pltpu.make_async_copy(
-                    result_out.at[0, me], result_in.at[me], result_got.at[me]
-                ).start()
-
-            @pl.when(seq != me)
-            def _():
-                remote(
-                    result_out.at[0, seq],
-                    result_in.at[me],
-                    result_sent.at[0, seq],
-                    result_got.at[me],
-                    device(seq, owner_chan),
-                ).start()
-
-            return carry
-
-        lax.fori_loop(0, n_seq, send_result, 0)
+    targets = (mixed_hbm, query_grad_hbm, key_grad_hbm, value_grad_hbm)
+    filter_store = pltpu.make_async_copy(filter_grad_ref, filter_grad_hbm, output_sent.at[4])
+
+    @pl.when(is_owner)
+    def _():
+        filter_store.start()
 
     def finish_block(step, carry):
-        source = (me + n_seq // 2 + n_seq - step) % n_seq
+        source = (me + n_seq // 2 + step) % n_seq
         block = owner_of(source)
         lanes = lanes_of(block)
         await_on(result_in.at[block], result_got.at[block])
@@ -421,17 +456,21 @@
         mix = result_in[block, 0:rows, :].astype(F32)
         back = result_in[block, rows : 2 * rows, :].astype(F32)
         spare = jnp.zeros((6, BLOCK), F32)
-        mixed_ref[:, lanes] = (shorted[0, 0:rows, lanes] * mix).astype(BF16)
+        outputs[0, :, lanes] = (shorted[0, 0:rows, lanes] * mix).astype(BF16)
         mix = jnp.concatenate([mix, edge[0:2], spare], 0)
         back = jnp.concatenate([back, edge[2:4], spare], 0)
         gated[0] = extended[3, 8 : rows + 16, lanes] * mix
         gated[1] = back * shorted[2, :, lanes]
         gated[2] = back * shorted[1, :, lanes]
-        for p, target in enumerate((query_grad_ref, key_grad_ref, value_grad_ref)):
+        for p in range(3):
             total = taps_ref[p, 0:1, lanes] * gated[p, 0:rows, :]
             total += taps_ref[p, 1:2, lanes] * gated[p, 1 : rows + 1, :]
             total += taps_ref[p, 2:3, lanes] * gated[p, 2 : rows + 2, :]
-            target[:, lanes] = total.astype(BF16)
+            outputs[p + 1, :, lanes] = total.astype(BF16)
+        for p, target in enumerate(targets):
+            pltpu.make_async_copy(
+                outputs.at[p, :, lanes], target.at[:, lanes], output_sent.at[p]
+            ).start()
         return carry
 
     lax.fori_loop(0, n_seq, finish_block, 0)
@@ -440,6 +479,7 @@
     def _():
         await_on(terms_in, single_got.at[2])
         filter_grad_ref[...] = terms_in[...].astype(F32)
+        filter_store.start()
         filter_copy.wait_send()
         skip_copy.wait_send()
 
@@ -450,6 +490,10 @@
     @pl.when(me > 0)
     def _():
         to_previous.wait_send()
+
+    for p, target in enumerate(targets):
+        pltpu.make_async_copy(outputs.at[p], target, output_sent.at[p]).wait()
+    filter_store.wait()
 
     def drain_block(block, carry):
         @pl.when(jnp.logical_or(not_owner, block != me))
@@ -474,6 +518,18 @@
             return carry
 
         lax.fori_loop(0, n_seq, drain_result, 0)
+
+
+def hand_over(*refs):
+    sources, targets, done = refs[:5], refs[5:10], refs[10]
+    copies = [
+        pltpu.make_async_copy(source, target, done.at[index])
+        for index, (source, target) in enumerate(zip(sources, targets))
+    ]
+    for copy in copies:
+        copy.start()
+    for copy in copies:
+        copy.wait()
 
 
 def dense_device(
@@ -486,12 +542,16 @@
     sequence_like = jax.ShapeDtypeStruct((rows, width), BF16)
     wide = 2 * channels
     semaphores = pltpu.SemaphoreType.DMA
-    return pl.pallas_call(
+    results = pl.pallas_call(
         functools.partial(dense_kernel, n_seq, n_chan),
         out_shape=(sequence_like,) * 4 + (jax.ShapeDtypeStruct((channels, length), F32),),
-        in_specs=[whole] * 7 + [apart] * 2,
-        out_specs=(whole,) * 5,
+        in_specs=[apart] * 3 + [whole] * 2 + [apart] * 4,
+        out_specs=(apart,) * 5,
         scratch_shapes=[
+            pltpu.VMEM((4, rows, width), BF16),
+            pltpu.VMEM((channels, length), F32),
+            pltpu.VMEM((4, rows, width), BF16),
+            pltpu.VMEM((channels, length), F32),
             pltpu.VMEM((2 * length, length), BF16),
             pltpu.VMEM((length, 2 * length), BF16),
             pltpu.VMEM((4, rows + 16, width), F32),
@@ -513,6 +573,7 @@
             pltpu.VMEM((wide, length), BF16),
             pltpu.VMEM((wide, length), BF16),
             pltpu.VMEM((wide, 2 * length), BF16),
+            pltpu.VMEM((2 * length, wide), F32),
             semaphores((2,)),
             semaphores((2,)),
             semaphores((n_seq,)),
@@ -522,6 +583,8 @@
             semaphores((3,)),
             semaphores((3,)),
             semaphores((2,)),
+            semaphores((5,)),
+            semaphores((5,)),
         ],
         compiler_params=pltpu.CompilerParams(
             collective_id=0, has_side_effects=True, vmem_limit_bytes=56 * 1024 * 1024
@@ -536,6 +599,14 @@
         cotangent,
         *[jnp.asarray(table) for table in tables],
     )
+    return pl.pallas_call(
+        hand_over,
+        out_shape=[jax.ShapeDtypeStruct(result.shape, result.dtype) for result in results],
+        in_specs=[apart] * 5,
+        out_specs=[apart] * 5,
+        scratch_shapes=[semaphores((5,))],
+        compiler_params=pltpu.CompilerParams(vmem_limit_bytes=56 * 1024 * 1024),
+    )(*results)
 
 
 exact_mode = lax.Precision.HIGHEST
@@ -752,7 +823,7 @@
             and length <= 1024
         ):
             tables = transform_tables(length)
-            return dense_device(n_seq, n_chan, tables, *arguments)
+            return tuple(dense_device(n_seq, n_chan, tables, *arguments))
         return per_device(*arguments)
 
     return jax.shard_map(

time: 65.9 us -> 103 us (1.56)
  the two profiles are of different devices: /device:TPU:0 before, /device:TPU:17 now
where the time goes in v1:
time: 103 us
  Pallas kernels  102 us (99%)
    pallas_call x1, Pallas kernels, dense_device(): pl.pallas_call(functools.partial(dense_kernel, n_seq, n_chan), out_shape=...  53.6 us
    pallas_call x1, Pallas kernels, dense_device(): pl.pallas_call(hand_over, out_shape=[jax.ShapeDtypeStruct(result.shape, r...  48.8 us

profile of v1, /device:TPU:17, one launch (start us, length us, event | category | flops | bytes accessed | tf_op | source)
XLA Modules:
  0.0 103.0 jit_solution(275304821959755081)
XLA Ops:
  0.6 53.6 %shard_map.128 = (bf16[128,1024]{1,0:T(8,128)(2,1)}, bf16[128,1024]{1,0:T(8,128)(2,1)}, bf16[128,1024]{1,0:T(8,128)(2,1)}, bf16[128,1024]{1,0:T(8,128)(2,1)}, f32[128,1024]{1,0:T(8,128)}) custom-call(bf16[128,1024]{1,0:T(8,128)(2,1)} %query_hbm.1, bf16[128,1024]{1,0:T(8,128)(2,1)} %key_hbm.1, bf16[128,1024]{1,0:T(8,128)(2,1)} %value_hbm.1, ...), custom_call_target="tpu_custom_call" | custom-call | tf_op jit(solution)/shard_map/pallas_call | solution.py:545
  54.2 48.8 %shard_map.129 = (bf16[128,1024]{1,0:T(8,128)(2,1)}, bf16[128,1024]{1,0:T(8,128)(2,1)}, bf16[128,1024]{1,0:T(8,128)(2,1)}, bf16[128,1024]{1,0:T(8,128)(2,1)}, f32[128,1024]{1,0:T(8,128)}) custom-call(bf16[128,1024]{1,0:T(8,128)(2,1)} %get-tuple-element.10.refs_0_, bf16[128,1024]{1,0:T(8,128)(2,1)} %get-tuple-element.11.refs_1_, ...), custom_call_target="tpu_custom_call" | custom-call | tf_op jit(solution)/shard_map/pallas_call | solution.py:602

commit v2 on v1

--- a/solution.py
+++ b/solution.py
@@ -521,15 +521,21 @@
 
 
 def hand_over(*refs):
-    sources, targets, done = refs[:5], refs[5:10], refs[10]
-    copies = [
-        pltpu.make_async_copy(source, target, done.at[index])
-        for index, (source, target) in enumerate(zip(sources, targets))
+    sources, targets, held = refs[:5], refs[5:10], refs[10:15]
+    loaded, stored = refs[15], refs[16]
+    loads = [
+        pltpu.make_async_copy(sources[index], held[index], loaded.at[index]) for index in range(5)
     ]
-    for copy in copies:
-        copy.start()
-    for copy in copies:
-        copy.wait()
+    stores = [
+        pltpu.make_async_copy(held[index], targets[index], stored.at[index]) for index in range(5)
+    ]
+    for load in loads:
+        load.start()
+    for load, store in zip(loads, stores):
+        load.wait()
+        store.start()
+    for store in stores:
+        store.wait()
 
 
 def dense_device(
@@ -604,7 +610,8 @@
         out_shape=[jax.ShapeDtypeStruct(result.shape, result.dtype) for result in results],
         in_specs=[apart] * 5,
         out_specs=[apart] * 5,
-        scratch_shapes=[semaphores((5,))],
+        scratch_shapes=[pltpu.VMEM(result.shape, result.dtype) for result in results]
+        + [semaphores((5,)), semaphores((5,))],
         compiler_params=pltpu.CompilerParams(vmem_limit_bytes=56 * 1024 * 1024),
     )(*results)
 

time: 103 us -> 56.7 us (0.55)
  Pallas kernels: 102 us -> 55.8 us
    pallas_call x1, Pallas kernels: 48.8 us -> 2.24 us  [dense_device(): pl.pallas_call(hand_over, out_shape=[jax.ShapeDtypeStruct(result.shape, r...]
where the time goes in v2:
time: 56.7 us; the launch traced here: 56.5 us
  Pallas kernels  55.8 us (98%)
  between operations  0.64 us (1%)
    pallas_call x1, Pallas kernels, dense_device(): pl.pallas_call(functools.partial(dense_kernel, n_seq, n_chan), out_shape=...  53.6 us
    pallas_call x1, Pallas kernels, dense_device(): pl.pallas_call(hand_over, out_shape=[jax.ShapeDtypeStruct(result.shape, r...  2.24 us

profile of v2, /device:TPU:17, one launch (start us, length us, event | category | flops | bytes accessed | tf_op | source)
XLA Modules:
  0.0 56.5 jit_solution(9189376129161799009)
XLA Ops:
  0.6 53.6 %shard_map.128 = (bf16[128,1024]{1,0:T(8,128)(2,1)}, bf16[128,1024]{1,0:T(8,128)(2,1)}, bf16[128,1024]{1,0:T(8,128)(2,1)}, bf16[128,1024]{1,0:T(8,128)(2,1)}, f32[128,1024]{1,0:T(8,128)}) custom-call(bf16[128,1024]{1,0:T(8,128)(2,1)} %query_hbm.1, bf16[128,1024]{1,0:T(8,128)(2,1)} %key_hbm.1, bf16[128,1024]{1,0:T(8,128)(2,1)} %value_hbm.1, ...), custom_call_target="tpu_custom_call" | custom-call | tf_op jit(solution)/shard_map/pallas_call | solution.py:551
  54.2 2.2 %shard_map.129 = (bf16[128,1024]{1,0:T(8,128)(2,1)}, bf16[128,1024]{1,0:T(8,128)(2,1)}, bf16[128,1024]{1,0:T(8,128)(2,1)}, bf16[128,1024]{1,0:T(8,128)(2,1)}, f32[128,1024]{1,0:T(8,128)}) custom-call(bf16[128,1024]{1,0:T(8,128)(2,1)} %get-tuple-element.10.refs_0_, bf16[128,1024]{1,0:T(8,128)(2,1)} %get-tuple-element.11.refs_1_, ...), custom_call_target="tpu_custom_call" | custom-call | tf_op jit(solution)/shard_map/pallas_call | solution.py:608

commit v3 on v2

--- a/solution.py
+++ b/solution.py
@@ -54,8 +54,10 @@
     halo_in,
     block_out,
     block_in,
-    result_out,
-    result_in,
+    mix_out,
+    back_out,
+    mix_in,
+    back_in,
     filter_out,
     filter_in,
     skip_in,
@@ -224,51 +226,55 @@
     def owner_of(block):
         return jnp.where(is_owner, block, n_seq - 1 - block)
 
-    def send_block(step, carry):
-        block = (me + n_seq // 2 + step) % n_seq
-        lanes = lanes_of(block)
-        for p in range(3):
-            total = taps_ref[p, 0:1, lanes] * extended[p, 8 : rows + 16, lanes]
-            total += taps_ref[p, 1:2, lanes] * extended[p, 7 : rows + 15, lanes]
-            total += taps_ref[p, 2:3, lanes] * extended[p, 6 : rows + 14, lanes]
-            shorted[p, :, lanes] = total.astype(BF16).astype(F32)
-        product = shorted[1, 0:rows, lanes] * shorted[2, 0:rows, lanes]
-        block_out[block, 0:rows, :] = product.astype(BF16)
-        gate = extended[3, 8 : rows + 8, lanes] * shorted[0, 0:rows, lanes]
-        block_out[block, rows : 2 * rows, :] = gate.astype(BF16)
-        target = owner_of(block)
+    def shorten(p, lanes):
+        total = taps_ref[p, 0:1, lanes] * extended[p, 8 : rows + 16, lanes]
+        total += taps_ref[p, 1:2, lanes] * extended[p, 7 : rows + 15, lanes]
+        total += taps_ref[p, 2:3, lanes] * extended[p, 6 : rows + 14, lanes]
+        shorted[p, :, lanes] = total.astype(BF16).astype(F32)
+
+    def send_block(kind, block):
         here = jnp.logical_and(is_owner, block == me)
 
         @pl.when(here)
         def _():
             pltpu.make_async_copy(
-                block_out.at[block], block_in.at[0, me], block_got.at[0, me]
+                block_out.at[kind, block], block_in.at[kind, 0, me], block_got.at[kind, 0, me]
             ).start()
 
         @pl.when(jnp.logical_not(here))
         def _():
             remote(
-                block_out.at[block],
-                block_in.at[side, me],
-                block_sent.at[block],
-                block_got.at[side, me],
-                device(target, owner_chan),
+                block_out.at[kind, block],
+                block_in.at[kind, side, me],
+                block_sent.at[kind, block],
+                block_got.at[kind, side, me],
+                device(owner_of(block), owner_chan),
             ).start()
 
+    def send_input(step, carry):
+        block = (me + n_seq // 2 + step) % n_seq
+        lanes = lanes_of(block)
+        shorten(1, lanes)
+        shorten(2, lanes)
+        product = shorted[1, 0:rows, lanes] * shorted[2, 0:rows, lanes]
+        block_out[0, block] = product.astype(BF16)
+        send_block(0, block)
         return carry
 
-    lax.fori_loop(0, n_seq, send_block, 0)
-
-    def columns_of(seq):
-        return jnp.concatenate(
-            [
-                block_in[0, seq, 0:rows, :],
-                block_in[1, seq, 0:rows, :],
-                block_in[0, seq, rows : 2 * rows, :],
-                block_in[1, seq, rows : 2 * rows, :],
-            ],
-            1,
-        )
+    def send_gate(step, carry):
+        block = (me + n_seq // 2 + step) % n_seq
+        lanes = lanes_of(block)
+        shorten(0, lanes)
+        gate = extended[3, 8 : rows + 8, lanes] * shorted[0, 0:rows, lanes]
+        block_out[1, block] = gate.astype(BF16)
+        send_block(1, block)
+        return carry
+
+    lax.fori_loop(0, n_seq, send_input, 0)
+    lax.fori_loop(0, n_seq, send_gate, 0)
+
+    def columns_of(kind, seq):
+        return jnp.concatenate([block_in[kind, 0, seq], block_in[kind, 1, seq]], 1)
 
     wide = 2 * BLOCK
 
@@ -312,105 +318,134 @@
 
         lax.fori_loop(0, chunks, kernel_transform, 0)
 
-        for step in range(chunks):
-            piece = (me // 2 + step) % chunks
-            for half in range(2):
-                for from_side in range(2):
-                    seq = 2 * piece + half
-                    await_on(block_in.at[from_side, seq], block_got.at[from_side, seq])
-            columns = jnp.concatenate([columns_of(2 * piece), columns_of(2 * piece + 1)], 0)
-            lags = pl.ds(pl.multiple_of(piece * chunk, chunk), chunk)
-
-            def transform(index, carry):
-                at = pl.ds(pl.multiple_of(index * chunk, chunk), chunk)
-                term = jnp.dot(forward[at, lags], columns, preferred_element_type=F32)
-                if step == 0:
-                    spectra[at, :] = term
-                else:
-                    spectra[at, :] += term
-                return carry
-
-            lax.fori_loop(0, 2 * chunks, transform, 0)
-
-        def spectral_products(index, carry):
+        def transform_blocks(kind):
+            lanes = slice(kind * wide, (kind + 1) * wide)
+            for step in range(chunks):
+                piece = (me // 2 + step) % chunks
+                for half in range(2):
+                    for from_side in range(2):
+                        seq = 2 * piece + half
+                        await_on(
+                            block_in.at[kind, from_side, seq], block_got.at[kind, from_side, seq]
+                        )
+                columns = jnp.concatenate(
+                    [columns_of(kind, 2 * piece), columns_of(kind, 2 * piece + 1)], 0
+                )
+                lags = pl.ds(pl.multiple_of(piece * chunk, chunk), chunk)
+
+                def transform(index, carry):
+                    at = pl.ds(pl.multiple_of(index * chunk, chunk), chunk)
+                    term = jnp.dot(forward[at, lags], columns, preferred_element_type=F32)
+                    if step == 0:
+                        spectra[at, lanes] = term
+                    else:
+                        spectra[at, lanes] += term
+                    return carry
+
+                lax.fori_loop(0, 2 * chunks, transform, 0)
+
+        def mix_products(index, carry):
             first, second = halves(index)
             kernel_cos, kernel_sin = kernel_spectra[first, :], kernel_spectra[second, :]
             input_cos, input_sin = spectra[first, 0:wide], spectra[second, 0:wide]
-            grad_cos, grad_sin = spectra[first, wide:], spectra[second, wide:]
             mix_cos = kernel_cos * input_cos - kernel_sin * input_sin
             mix_sin = kernel_cos * input_sin + kernel_sin * input_cos
+            products[first, 0:wide] = mix_cos.astype(BF16)
+            products[second, 0:wide] = mix_sin.astype(BF16)
+            return carry
+
+        def back_products(index, carry):
+            first, second = halves(index)
+            kernel_cos, kernel_sin = kernel_spectra[first, :], kernel_spectra[second, :]
+            grad_cos, grad_sin = spectra[first, wide:], spectra[second, wide:]
             back_cos = kernel_cos * grad_cos + kernel_sin * grad_sin
             back_sin = kernel_cos * grad_sin - kernel_sin * grad_cos
-            products[first, 0:wide] = mix_cos.astype(BF16)
-            products[second, 0:wide] = mix_sin.astype(BF16)
             products[first, wide:] = back_cos.astype(BF16)
             products[second, wide:] = back_sin.astype(BF16)
             return carry
 
-        lax.fori_loop(0, chunks, spectral_products, 0)
-        await_on(skip_in, single_got.at[1])
-        gains = [skip_ref[pl.ds(me, 1), :], skip_in[pl.ds(mirrored_seq, 1), :]]
-        gains = jnp.concatenate(gains + gains, 1)
-        inverse_copy.wait()
-
-        def send_result(seq):
+        def send_result(kind, source, target, seq):
             remote(
-                result_out.at[1, seq],
-                result_in.at[mirrored_seq],
-                result_sent.at[1, seq],
-                result_got.at[mirrored_seq],
+                source.at[1, seq],
+                target.at[mirrored_seq],
+                result_sent.at[kind, 1, seq],
+                result_got.at[kind, mirrored_seq],
                 device(seq, other_chan),
             ).start()
 
             @pl.when(seq == me)
             def _():
                 pltpu.make_async_copy(
-                    result_out.at[0, me], result_in.at[me], result_got.at[me]
+                    source.at[0, me], target.at[me], result_got.at[kind, me]
                 ).start()
 
             @pl.when(seq != me)
             def _():
                 remote(
-                    result_out.at[0, seq],
-                    result_in.at[me],
-                    result_sent.at[0, seq],
-                    result_got.at[me],
+                    source.at[0, seq],
+                    target.at[me],
+                    result_sent.at[kind, 0, seq],
+                    result_got.at[kind, me],
                     device(seq, owner_chan),
                 ).start()
 
         first_piece = (me // 2 + chunks // 2) % chunks
-        for to_side in range(2):
-            result_out[to_side, n_seq - 1, 2 * rows :, :] = jnp.zeros((16, BLOCK), BF16)
-
-        def results(step, carry):
+
+        def sums_of(kind, index):
+            at = pl.ds(pl.multiple_of(index * chunk, chunk), chunk)
+            lanes = slice(kind * wide, (kind + 1) * wide)
+            return jnp.dot(inverse[at, :], products[:, lanes], preferred_element_type=F32) * scale
+
+        def mix_results(step, carry):
             index = (first_piece + chunks - step) % chunks
-            at = pl.ds(pl.multiple_of(index * chunk, chunk), chunk)
-            sums = jnp.dot(inverse[at, :], products[...], preferred_element_type=F32) * scale
+            sums = sums_of(0, index)
             for half in range(2):
                 seq = 2 * index + half
                 here = sums[half * rows : (half + 1) * rows]
-                here = here + gains * columns_of(seq).astype(F32)
+                here = here + gains * columns_of(0, seq).astype(F32)
+                mix_out[0, seq] = here[:, 0:BLOCK].astype(BF16)
+                mix_out[1, seq] = here[:, BLOCK:].astype(BF16)
+                send_result(0, mix_out, mix_in, seq)
+            return carry
+
+        def back_results(step, carry):
+            index = (first_piece + chunks - step) % chunks
+            sums = sums_of(1, index)
+            for half in range(2):
+                seq = 2 * index + half
+                here = sums[half * rows : (half + 1) * rows]
+                here = here + gains * columns_of(1, seq).astype(F32)
                 before = (seq + n_seq - 1) % n_seq
                 for to_side in range(2):
-                    mix = here[:, to_side * BLOCK : (to_side + 1) * BLOCK]
-                    back = here[:, wide + to_side * BLOCK : wide + (to_side + 1) * BLOCK]
-                    result_out[to_side, seq, 0:rows, :] = mix.astype(BF16)
-                    result_out[to_side, seq, rows : 2 * rows, :] = back.astype(BF16)
+                    back = here[:, to_side * BLOCK : (to_side + 1) * BLOCK]
+                    back_out[to_side, seq, 0:rows, :] = back.astype(BF16)
+                    mix = mix_out[to_side, seq, 0:16, :].astype(F32)
                     edge = jnp.concatenate([mix[0:2], back[0:2], jnp.zeros((12, BLOCK), F32)], 0)
 
                     @pl.when(seq > 0)
                     def _():
-                        result_out[to_side, before, 2 * rows :, :] = edge.astype(BF16)
+                        back_out[to_side, before, rows:, :] = edge.astype(BF16)
 
             @pl.when(step > 0)
             def _():
-                send_result(2 * index + 1)
-
-            send_result(2 * index)
+                send_result(1, back_out, back_in, 2 * index + 1)
+
+            send_result(1, back_out, back_in, 2 * index)
             return carry
 
-        lax.fori_loop(0, chunks, results, 0)
-        send_result(2 * first_piece + 1)
+        for to_side in range(2):
+            back_out[to_side, n_seq - 1, rows:, :] = jnp.zeros((16, BLOCK), BF16)
+        await_on(skip_in, single_got.at[1])
+        gains = [skip_ref[pl.ds(me, 1), :], skip_in[pl.ds(mirrored_seq, 1), :]]
+        gains = jnp.concatenate(gains, 1)
+        transform_blocks(0)
+        lax.fori_loop(0, chunks, mix_products, 0)
+        inverse_copy.wait()
+        lax.fori_loop(0, chunks, mix_results, 0)
+        transform_blocks(1)
+        lax.fori_loop(0, chunks, back_products, 0)
+        lax.fori_loop(0, chunks, back_results, 0)
+        send_result(1, back_out, back_in, 2 * first_piece + 1)
 
         def lag_products(index, carry):
             first, second = halves(index)
@@ -447,18 +482,27 @@
     def _():
         filter_store.start()
 
+    def store_block(p, lanes):
+        pltpu.make_async_copy(
+            outputs.at[p, :, lanes], targets[p].at[:, lanes], output_sent.at[p]
+        ).start()
+
+    def finish_mix(step, carry):
+        block = owner_of((me + n_seq // 2 + step) % n_seq)
+        lanes = lanes_of(block)
+        await_on(mix_in.at[block], result_got.at[0, block])
+        outputs[0, :, lanes] = (shorted[0, 0:rows, lanes] * mix_in[block].astype(F32)).astype(BF16)
+        store_block(0, lanes)
+        return carry
+
     def finish_block(step, carry):
-        source = (me + n_seq // 2 + step) % n_seq
-        block = owner_of(source)
+        block = owner_of((me + n_seq // 2 + step) % n_seq)
         lanes = lanes_of(block)
-        await_on(result_in.at[block], result_got.at[block])
-        edge = result_in[block, 2 * rows :, :].astype(F32)
-        mix = result_in[block, 0:rows, :].astype(F32)
-        back = result_in[block, rows : 2 * rows, :].astype(F32)
+        await_on(back_in.at[block], result_got.at[1, block])
+        edge = back_in[block, rows:, :].astype(F32)
         spare = jnp.zeros((6, BLOCK), F32)
-        outputs[0, :, lanes] = (shorted[0, 0:rows, lanes] * mix).astype(BF16)
-        mix = jnp.concatenate([mix, edge[0:2], spare], 0)
-        back = jnp.concatenate([back, edge[2:4], spare], 0)
+        mix = jnp.concatenate([mix_in[block].astype(F32), edge[0:2], spare], 0)
+        back = jnp.concatenate([back_in[block, 0:rows, :].astype(F32), edge[2:4], spare], 0)
         gated[0] = extended[3, 8 : rows + 16, lanes] * mix
         gated[1] = back * shorted[2, :, lanes]
         gated[2] = back * shorted[1, :, lanes]
@@ -467,12 +511,10 @@
             total += taps_ref[p, 1:2, lanes] * gated[p, 1 : rows + 1, :]
             total += taps_ref[p, 2:3, lanes] * gated[p, 2 : rows + 2, :]
             outputs[p + 1, :, lanes] = total.astype(BF16)
-        for p, target in enumerate(targets):
-            pltpu.make_async_copy(
-                outputs.at[p, :, lanes], target.at[:, lanes], output_sent.at[p]
-            ).start()
+            store_block(p + 1, lanes)
         return carry
 
+    lax.fori_loop(0, n_seq, finish_mix, 0)
     lax.fori_loop(0, n_seq, finish_block, 0)
 
     @pl.when(not_owner)
@@ -498,7 +540,8 @@
     def drain_block(block, carry):
         @pl.when(jnp.logical_or(not_owner, block != me))
         def _():
-            await_on(block_out.at[block], block_sent.at[block])
+            for kind in range(2):
+                await_on(block_out.at[kind, block], block_sent.at[kind, block])
 
         return carry
 
@@ -509,11 +552,13 @@
         terms_copy.wait_send()
 
         def drain_result(seq, carry):
-            await_on(result_out.at[1, seq], result_sent.at[1, seq])
+            for kind, source in enumerate((mix_out, back_out)):
+                await_on(source.at[1, seq], result_sent.at[kind, 1, seq])
 
             @pl.when(seq != me)
             def _():
-                await_on(result_out.at[0, seq], result_sent.at[0, seq])
+                for kind, source in enumerate((mix_out, back_out)):
+                    await_on(source.at[0, seq], result_sent.at[kind, 0, seq])
 
             return carry
 
@@ -565,10 +610,12 @@
             pltpu.VMEM((3, rows + 8, channels), F32),
             pltpu.VMEM((2, 8, width), F32),
             pltpu.VMEM((2, 8, width), F32),
-            pltpu.VMEM((n_seq, 2 * rows, channels), BF16),
-            pltpu.VMEM((2, n_seq, 2 * rows, channels), BF16),
-            pltpu.VMEM((2, n_seq, 2 * rows + 16, channels), BF16),
-            pltpu.VMEM((n_seq, 2 * rows + 16, channels), BF16),
+            pltpu.VMEM((2, n_seq, rows, channels), BF16),
+            pltpu.VMEM((2, 2, n_seq, rows, channels), BF16),
+            pltpu.VMEM((2, n_seq, rows, channels), BF16),
+            pltpu.VMEM((2, n_seq, rows + 16, channels), BF16),
+            pltpu.VMEM((n_seq, rows, channels), BF16),
+            pltpu.VMEM((n_seq, rows + 16, channels), BF16),
             pltpu.VMEM((channels, length), BF16),
             pltpu.VMEM((channels, length), BF16),
             pltpu.VMEM((n_seq, channels), F32),
@@ -582,10 +629,10 @@
             pltpu.VMEM((2 * length, wide), F32),
             semaphores((2,)),
             semaphores((2,)),
-            semaphores((n_seq,)),
             semaphores((2, n_seq)),
+            semaphores((2, 2, n_seq)),
+            semaphores((2, 2, n_seq)),
             semaphores((2, n_seq)),
-            semaphores((n_seq,)),
             semaphores((3,)),
             semaphores((3,)),
             semaphores((2,)),

time: 56.7 us -> 58 us (1.023)
  Pallas kernels: 55.8 us -> 57.2 us
    pallas_call x1, Pallas kernels: 53.6 us -> 54.9 us  [dense_device(): pl.pallas_call(functools.partial(dense_kernel, n_seq, n_chan), out_shape=...]
where the time goes in v3:
time: 58 us; the launch traced here: 57.8 us
  Pallas kernels  57.2 us (99%)
  between operations  0.64 us (1%)
    pallas_call x1, Pallas kernels, dense_device(): pl.pallas_call(functools.partial(dense_kernel, n_seq, n_chan), out_shape=...  54.9 us
    pallas_call x1, Pallas kernels, dense_device(): pl.pallas_call(hand_over, out_shape=[jax.ShapeDtypeStruct(result.shape, r...  2.24 us

profile of v3, /device:TPU:17, one launch (start us, length us, event | category | flops | bytes accessed | tf_op | source)
XLA Modules:
  0.0 57.8 jit_solution(15219341901900204147)
XLA Ops:
  0.6 54.9 %shard_map.128 = (bf16[128,1024]{1,0:T(8,128)(2,1)}, bf16[128,1024]{1,0:T(8,128)(2,1)}, bf16[128,1024]{1,0:T(8,128)(2,1)}, bf16[128,1024]{1,0:T(8,128)(2,1)}, f32[128,1024]{1,0:T(8,128)}) custom-call(bf16[128,1024]{1,0:T(8,128)(2,1)} %query_hbm.1, bf16[128,1024]{1,0:T(8,128)(2,1)} %key_hbm.1, bf16[128,1024]{1,0:T(8,128)(2,1)} %value_hbm.1, ...), custom_call_target="tpu_custom_call" | custom-call | tf_op jit(solution)/shard_map/pallas_call | solution.py:596
  55.6 2.2 %shard_map.129 = (bf16[128,1024]{1,0:T(8,128)(2,1)}, bf16[128,1024]{1,0:T(8,128)(2,1)}, bf16[128,1024]{1,0:T(8,128)(2,1)}, bf16[128,1024]{1,0:T(8,128)(2,1)}, f32[128,1024]{1,0:T(8,128)}) custom-call(bf16[128,1024]{1,0:T(8,128)(2,1)} %get-tuple-element.10.refs_0_, bf16[128,1024]{1,0:T(8,128)(2,1)} %get-tuple-element.11.refs_1_, ...), custom_call_target="tpu_custom_call" | custom-call | tf_op jit(solution)/shard_map/pallas_call | solution.py:655

commit v4 on v2

--- a/solution.py
+++ b/solution.py
@@ -78,6 +78,8 @@
     table_got,
     argument_got,
     output_sent,
+    terms_sent,
+    terms_got,
 ):
     rows = query_hbm.shape[0]
     length = filter_hbm.shape[1]
@@ -188,9 +190,15 @@
     skip_copy = remote(
         skip_ref, skip_in, single_sent.at[1], single_got.at[1], device(mirrored_seq, owner_chan)
     )
-    terms_copy = remote(
-        terms_out, terms_in, single_sent.at[2], single_got.at[2], device(mirrored_seq, other_chan)
-    )
+
+    def terms_copy(index):
+        return remote(
+            terms_out.at[index],
+            terms_in.at[index],
+            terms_sent.at[index],
+            terms_got.at[index],
+            device(mirrored_seq, other_chan),
+        )
 
     @pl.when(not_owner)
     def _():
@@ -433,12 +441,12 @@
             )
             ahead = cosine - sine
             behind = (cosine + sine).astype(BF16)
-            terms_out[:, lags] = ((ahead[BLOCK:] + flipped(behind[:BLOCK])) * scale).astype(BF16)
+            terms_out[index] = ((ahead[BLOCK:] + flipped(behind[:BLOCK])) * scale).astype(BF16)
+            terms_copy(index).start()
             filter_grad_ref[:, lags] = (ahead[:BLOCK] + flipped(behind[BLOCK:])) * scale
             return carry
 
         lax.fori_loop(0, chunks, filter_terms, 0)
-        terms_copy.start()
 
     targets = (mixed_hbm, query_grad_hbm, key_grad_hbm, value_grad_hbm)
     filter_store = pltpu.make_async_copy(filter_grad_ref, filter_grad_hbm, output_sent.at[4])
@@ -477,8 +485,10 @@
 
     @pl.when(not_owner)
     def _():
-        await_on(terms_in, single_got.at[2])
-        filter_grad_ref[...] = terms_in[...].astype(F32)
+        for index in range(chunks):
+            lags = slice(index * chunk, (index + 1) * chunk)
+            await_on(terms_in.at[index], terms_got.at[index])
+            filter_grad_ref[:, lags] = terms_in[index].astype(F32)
         filter_store.start()
         filter_copy.wait_send()
         skip_copy.wait_send()
@@ -506,7 +516,8 @@
 
     @pl.when(is_owner)
     def _():
-        terms_copy.wait_send()
+        for index in range(chunks):
+            terms_copy(index).wait_send()
 
         def drain_result(seq, carry):
             await_on(result_out.at[1, seq], result_sent.at[1, seq])
@@ -572,8 +583,8 @@
             pltpu.VMEM((channels, length), BF16),
             pltpu.VMEM((channels, length), BF16),
             pltpu.VMEM((n_seq, channels), F32),
-            pltpu.VMEM((channels, length), BF16),
-            pltpu.VMEM((channels, length), BF16),
+            pltpu.VMEM((length // (2 * rows), channels, 2 * rows), BF16),
+            pltpu.VMEM((length // (2 * rows), channels, 2 * rows), BF16),
             pltpu.VMEM((2 * length, 2 * wide), F32),
             pltpu.VMEM((2 * length, 2 * wide), BF16),
             pltpu.VMEM((wide, length), BF16),
@@ -591,6 +602,8 @@
             semaphores((2,)),
             semaphores((5,)),
             semaphores((5,)),
+            semaphores((length // (2 * rows),)),
+            semaphores((length // (2 * rows),)),
         ],
         compiler_params=pltpu.CompilerParams(
             collective_id=0, has_side_effects=True, vmem_limit_bytes=56 * 1024 * 1024

time: 56.7 us -> 56.7 us (level)
  no operation moved by 1% of the time
where the time goes in v4:
time: 56.7 us; the launch traced here: 56.5 us
  Pallas kernels  55.9 us (99%)
  between operations  0.64 us (1%)
    pallas_call x1, Pallas kernels, dense_device(): pl.pallas_call(functools.partial(dense_kernel, n_seq, n_chan), out_shape=...  53.6 us
    pallas_call x1, Pallas kernels, dense_device(): pl.pallas_call(hand_over, out_shape=[jax.ShapeDtypeStruct(result.shape, r...  2.24 us

profile of v4, /device:TPU:17, one launch (start us, length us, event | category | flops | bytes accessed | tf_op | source)
XLA Modules:
  0.0 56.5 jit_solution(5629645297555952497)
XLA Ops:
  0.6 53.6 %shard_map.128 = (bf16[128,1024]{1,0:T(8,128)(2,1)}, bf16[128,1024]{1,0:T(8,128)(2,1)}, bf16[128,1024]{1,0:T(8,128)(2,1)}, bf16[128,1024]{1,0:T(8,128)(2,1)}, f32[128,1024]{1,0:T(8,128)}) custom-call(bf16[128,1024]{1,0:T(8,128)(2,1)} %query_hbm.1, bf16[128,1024]{1,0:T(8,128)(2,1)} %key_hbm.1, bf16[128,1024]{1,0:T(8,128)(2,1)} %value_hbm.1, ...), custom_call_target="tpu_custom_call" | custom-call | tf_op jit(solution)/shard_map/pallas_call | solution.py:562
  54.3 2.2 %shard_map.129 = (bf16[128,1024]{1,0:T(8,128)(2,1)}, bf16[128,1024]{1,0:T(8,128)(2,1)}, bf16[128,1024]{1,0:T(8,128)(2,1)}, bf16[128,1024]{1,0:T(8,128)(2,1)}, f32[128,1024]{1,0:T(8,128)}) custom-call(bf16[128,1024]{1,0:T(8,128)(2,1)} %get-tuple-element.10.refs_0_, bf16[128,1024]{1,0:T(8,128)(2,1)} %get-tuple-element.11.refs_1_, ...), custom_call_target="tpu_custom_call" | custom-call | tf_op jit(solution)/shard_map/pallas_call | solution.py:621
